TPU v7x, 128 devices: a whole 4x4x4 slice. The times are simulated.
128 devices in a mesh: qa: 8 (over x, y_lo), qb: 16 (over y_hi, z, core).
Axes of the slice: x: 4, y: 4 (y_hi: 2, y_lo: 2; y = y_hi * 2 + y_lo), z: 4, core: 2. Of those that a mesh axis runs over, the one named last changes fastest.
Arguments:
- amplitudes: float32 [8, 16, 128, 128, 128], P('qa', 'qb'), may hold values from -6 to 6
- gates: float32 [2, 4, 128, 128], replicated, may hold values from -0.5 to 0.5
- qubit_order: int32 [2, 4, 7], replicated, may hold values from 0 to 6, each once within a row
Outputs:
- rotated: float32 [8, 16, 128, 128, 128], P('qa', 'qb')
Inputs may be any that keep to these rules, and one draw needn't show every extreme that they name: Each row of qubit_order lists every number 0 to 6 exactly once.
All inputs are finite; a program needn't handle non-finite values.
Results may differ from a plain program's by a relative error of at most 0.00011.
Values sent between devices are 32-bit elements; how exact they have to be, the bound alone decides.
No kernel may reach another device: no remote copies, remote signals or barrier semaphores. Data moves between devices by JAX's collectives and lax.ppermute only.
A program may use at most 128 MiB of HBM per device.

v0:
```python
import jax
import jax.numpy as jnp
from jax import lax
from jax.sharding import PartitionSpec as P

TURN = 3


def effective(matrix, qubit_seq):
    extent = matrix.shape[0]
    basis_index = jnp.arange(extent, dtype=jnp.int32)
    mapped = jnp.zeros_like(basis_index)
    for bit_pos in range(qubit_seq.shape[0]):
        mapped = mapped + jnp.left_shift(
            jnp.bitwise_and(jnp.right_shift(basis_index, qubit_seq[bit_pos]), 1), bit_pos
        )
    select = (mapped[:, None] == basis_index[None, :]).astype(jnp.float32)
    partial_gate = jnp.dot(
        select, matrix, precision=lax.Precision.HIGHEST, preferred_element_type=jnp.float32
    )
    return jnp.dot(
        partial_gate, select.T, precision=lax.Precision.HIGHEST, preferred_element_type=jnp.float32
    )


def group_product(state_grid, gate_matrix, outer_size):
    extent = state_grid.shape[-1]
    tiled_view = state_grid.reshape(outer_size, extent, -1)
    result = jnp.einsum(
        "ql,fln->fqn",
        gate_matrix,
        tiled_view,
        precision=lax.Precision.HIGHEST,
        preferred_element_type=jnp.float32,
    )
    return result.reshape(state_grid.shape)


def apply_front(state_grid, gate_matrix, shift_bits):
    return group_product(state_grid, gate_matrix, 2**shift_bits)


def apply_middle(state_grid, gate_matrix, shift_bits):
    if shift_bits == 0:
        return jnp.einsum(
            "mk,akc->amc",
            gate_matrix,
            state_grid,
            precision=lax.Precision.HIGHEST,
            preferred_element_type=jnp.float32,
        )
    turned = group_product(state_grid.transpose(1, 2, 0), gate_matrix, 2**shift_bits)
    return turned.transpose(2, 0, 1)


def apply_back(state_grid, gate_matrix, shift_bits):
    if shift_bits == 0:
        return jnp.einsum(
            "abk,mk->abm",
            state_grid,
            gate_matrix,
            precision=lax.Precision.HIGHEST,
            preferred_element_type=jnp.float32,
        )
    turned = group_product(state_grid.transpose(2, 0, 1), gate_matrix, 2**shift_bits)
    return turned.transpose(1, 2, 0)


def apply_rows(gate_matrix, pieces):
    flattened = pieces.reshape(gate_matrix.shape[0], -1)
    result = jnp.dot(
        gate_matrix, flattened, precision=lax.Precision.HIGHEST, preferred_element_type=jnp.float32
    )
    return result.reshape(pieces.shape)


def on_device(amplitudes, gates, qubit_order):
    state_grid = amplitudes.reshape(amplitudes.shape[2:])
    first_gates = [effective(gates[0, slot_idx], qubit_order[0, slot_idx]) for slot_idx in range(4)]
    second_gates = [
        effective(gates[1, slot_idx], qubit_order[1, slot_idx]) for slot_idx in range(4)
    ]
    state_grid = apply_front(state_grid, first_gates[0], 0)
    state_grid = apply_middle(state_grid, first_gates[1], 0)
    state_grid = apply_back(state_grid, first_gates[2], 0)
    state_grid = apply_rows(
        first_gates[3], lax.all_to_all(state_grid, "qa", split_axis=0, concat_axis=0, tiled=True)
    )
    state_grid = lax.all_to_all(state_grid, "qa", split_axis=0, concat_axis=0, tiled=True)
    state_grid = apply_front(state_grid, second_gates[0], TURN)
    state_grid = apply_middle(state_grid, second_gates[1], TURN)
    state_grid = apply_back(state_grid, second_gates[2], TURN)
    state_grid = apply_rows(
        second_gates[3], lax.all_to_all(state_grid, "qb", split_axis=0, concat_axis=0, tiled=True)
    )
    state_grid = lax.all_to_all(state_grid, "qb", split_axis=0, concat_axis=0, tiled=True)
    return state_grid.reshape(amplitudes.shape)


def solution(mesh):
    return jax.shard_map(
        on_device,
        mesh=mesh,
        in_specs=(P("qa", "qb", None, None, None), P(), P()),
        out_specs=P("qa", "qb", None, None, None),
        check_vma=False,
    )
```

profile of v0, /device:TPU:1, one launch (start us, length us, event | category | flops | bytes accessed | tf_op | source)
XLA Modules:
  0.0 780.6 jit_solution(8234439574403178264)
XLA Ops:
  0.0 2.1 fusion.52
  2.1 1.8 fusion.53
  3.8 4.5 shift-left_add_fusion.5
  8.4 1.1 fusion.20
  9.5 0.3 fusion.32
  9.7 16.1 %fusion.7 = f32[16,8,128,128]{3,1,2,0:T(8,128)S(1)} fusion(f32[128,128]{1,0:T(8,128)S(1)} %fusion.32, f32[16,8,128,128]{3,2,1,0:T(8,128)} %bitcast.166), kind=kOutput, calls=%fused_computation.11 | convolution fusion | flops 3221225472 | bytes 16842752 | tf_op jit(solution)/shard_map/ql,fln->fqn/dot_general | solution.py:29
  25.8 0.0 copy-start
  25.8 1.5 copy.52
  27.3 4.4 shift-left_add_fusion.4
  31.7 0.0 copy-done
  31.7 0.2 fusion.18
  31.9 0.3 convolution_bitcast_fusion.7
  32.2 4.3 shift-left_add_fusion.3
  36.5 0.2 fusion.16
  36.8 0.3 convolution_bitcast_fusion.6
  37.1 13.8 %fusion.54 = f32[128,128,128]{2,1,0:T(8,128)S(1)} fusion(f32[128,128,128]{2,1,0:T(8,128)S(1)} %bitcast.159, f32[128,128,1]{1,0,2:T(8,128)S(1)} %convolution_bitcast_fusion.7), kind=kOutput, calls=%fused_computation.79 | convolution fusion | flops 3221225472 | bytes 16842752 | tf_op jit(solution)/shard_map/mk,akc->amc/dot_general | solution.py:45
  50.8 15.8 %fusion.5 = f32[128,128,128]{2,1,0:T(8,128)} fusion(f32[128,128,1]{1,0,2:T(8,128)S(1)} %convolution_bitcast_fusion.6, f32[128,128,128]{2,1,0:T(8,128)S(1)} %fusion.54), kind=kOutput, calls=%fused_computation.6 | convolution fusion | flops 3221225472 | bytes 16842752 | tf_op jit(solution)/shard_map/abk,mk->abm/dot_general | solution.py:58
  66.6 6.4 all-to-all-start
  73.0 4.3 shift-left_add_fusion.6
  77.3 0.2 fusion.22
  77.6 0.3 convolution_bitcast_fusion.8
  77.8 110.2 %all-to-all-done = f32[128,128,128]{2,1,0:T(8,128)} async-done(((f32[128,128,128]{2,1,0:T(8,128)}), f32[128,128,128]{2,1,0:T(8,128)}, u32[]{:S(2)}, u32[]{:S(2)}) %all-to-all-start) | async-done | bytes 8388640 | tf_op jit(solution)/shard_map/all_to_all | solution.py:87
  188.0 13.3 %copy.61 = f32[16,8,128,128]{3,1,2,0:T(8,128)} copy(f32[16,8,128,128]{3,2,1,0:T(8,128)} %bitcast.97) | data formatting | bytes 16777216
  201.4 9.0 %copy.33 = f32[16384,128]{1,0:T(8,128)} copy(f32[16384,128]{0,1:T(8,128)} %bitcast.161) | data formatting | bytes 16777216 | tf_op jit(solution)/shard_map/dot_general | solution.py:71
  210.4 10.5 %fusion.55 = f32[128,128,128]{2,0,1:T(8,128)S(1)} fusion(f32[128,128,1]{1,0,2:T(8,128)S(1)} %convolution_bitcast_fusion.8, f32[128,128,128]{2,1,0:T(8,128)} %bitcast.160), kind=kOutput, calls=%fused_computation.80 | convolution fusion | flops 3221225472 | bytes 16842752 | tf_op jit(solution)/shard_map/dot_general | solution.py:71
  220.9 8.3 %copy.34 = f32[128,128,128]{2,1,0:T(8,128)} copy(f32[128,128,128]{2,0,1:T(8,128)S(1)} %fusion.55) | data formatting | bytes 16777216 | tf_op jit(solution)/shard_map/dot_general | solution.py:71
  229.1 5.1 all-to-all-start.1
  234.2 0.0 copy-done.1
  234.2 0.7 fusion.51
  235.0 4.2 shift-left_add_fusion.2
  239.2 4.4 shift-left_add_fusion.1
  243.6 4.3 shift-left_add_fusion
  247.9 0.2 fusion.14
  248.1 0.3 convolution_bitcast_fusion.5
  248.4 0.2 fusion.12
  248.6 0.3 convolution_bitcast_fusion.4
  248.9 0.2 fusion.10
  249.1 0.3 convolution_bitcast_fusion.3
  249.4 99.5 %all-to-all-done.1 = f32[128,128,128]{2,1,0:T(8,128)} async-done(((f32[128,128,128]{2,1,0:T(8,128)}), f32[128,128,128]{2,1,0:T(8,128)}, u32[]{:S(2)}, u32[]{:S(2)}) %all-to-all-start.1) | async-done | bytes 8388640 | tf_op jit(solution)/shard_map/all_to_all | solution.py:89
  348.9 9.2 %reshape.442 = f32[8,128,2048]{2,1,0:T(8,128)} reshape(f32[128,128,128]{2,1,0:T(8,128)} %all-to-all-done.1) | data formatting | bytes 16777216 | tf_op jit(solution)/shard_map/reshape | solution.py:28
  358.2 16.7 %convolution_bitcast_fusion.2 = f32[8,128,2048]{1,2,0:T(8,128)} fusion(f32[8,128,2048]{2,1,0:T(8,128)} %reshape.442, f32[128,128,1]{1,0,2:T(8,128)S(1)} %convolution_bitcast_fusion.5), kind=kOutput, calls=%fused_computation.10 | convolution fusion | flops 3221225472 | bytes 16842752 | tf_op jit(solution)/shard_map/ql,fln->fqn/dot_general | solution.py:29
  374.8 9.1 %copy.36 = f32[8,128,2048]{2,1,0:T(8,128)} copy(f32[8,128,2048]{1,2,0:T(8,128)} %convolution_bitcast_fusion.2) | data formatting | bytes 16777216 | tf_op jit(solution)/shard_map/ql,fln->fqn/transpose | solution.py:29
  384.0 9.3 %reshape.443 = f32[128,128,128]{2,1,0:T(8,128)} reshape(f32[8,128,2048]{2,1,0:T(8,128)} %copy.36) | data formatting | bytes 16777216 | tf_op jit(solution)/shard_map/reshape | solution.py:36
  393.2 9.3 %copy.37 = f32[128,128,128]{2,1,0:T(8,128)} copy(f32[128,128,128]{1,0,2:T(8,128)} %bitcast.162) | data formatting | bytes 16777216 | tf_op jit(solution)/shard_map/transpose | solution.py:52
  402.5 9.3 %reshape.444 = f32[8,128,2048]{2,1,0:T(8,128)} reshape(f32[128,128,128]{2,1,0:T(8,128)} %copy.37) | data formatting | bytes 16777216 | tf_op jit(solution)/shard_map/reshape | solution.py:28
  411.8 16.7 %convolution_bitcast_fusion.1 = f32[8,128,2048]{1,2,0:T(8,128)} fusion(f32[8,128,2048]{2,1,0:T(8,128)} %reshape.444, f32[128,128,1]{1,0,2:T(8,128)S(1)} %convolution_bitcast_fusion.4), kind=kOutput, calls=%fused_computation.9 | convolution fusion | flops 3221225472 | bytes 16842752 | tf_op jit(solution)/shard_map/ql,fln->fqn/dot_general | solution.py:29
  428.5 9.3 %copy.39 = f32[8,128,2048]{2,1,0:T(8,128)} copy(f32[8,128,2048]{1,2,0:T(8,128)} %convolution_bitcast_fusion.1) | data formatting | bytes 16777216 | tf_op jit(solution)/shard_map/ql,fln->fqn/transpose | solution.py:29
  437.7 9.2 %reshape.445 = f32[128,128,128]{2,1,0:T(8,128)} reshape(f32[8,128,2048]{2,1,0:T(8,128)} %copy.39) | data formatting | bytes 16777216 | tf_op jit(solution)/shard_map/reshape | solution.py:36
  447.0 9.3 %copy.40 = f32[128,128,128]{2,1,0:T(8,128)} copy(f32[128,128,128]{1,0,2:T(8,128)} %bitcast.163) | data formatting | bytes 16777216 | tf_op jit(solution)/shard_map/transpose;transpose | solution.py:65
  456.3 9.2 %reshape.446 = f32[8,128,2048]{2,1,0:T(8,128)} reshape(f32[128,128,128]{2,1,0:T(8,128)} %copy.40) | data formatting | bytes 16777216 | tf_op jit(solution)/shard_map/reshape | solution.py:28
  465.6 16.9 %convolution_bitcast_fusion = f32[8,128,2048]{1,2,0:T(8,128)} fusion(f32[8,128,2048]{2,1,0:T(8,128)} %reshape.446, f32[128,128,1]{1,0,2:T(8,128)S(1)} %convolution_bitcast_fusion.3), kind=kOutput, calls=%fused_computation.8 | convolution fusion | flops 3221225472 | bytes 16842752 | tf_op jit(solution)/shard_map/ql,fln->fqn/dot_general | solution.py:29
  482.4 9.1 %copy.42 = f32[8,128,2048]{2,1,0:T(8,128)} copy(f32[8,128,2048]{1,2,0:T(8,128)} %convolution_bitcast_fusion) | data formatting | bytes 16777216 | tf_op jit(solution)/shard_map/ql,fln->fqn/transpose | solution.py:29
  491.6 9.3 %reshape.447 = f32[128,128,128]{2,1,0:T(8,128)} reshape(f32[8,128,2048]{2,1,0:T(8,128)} %copy.42) | data formatting | bytes 16777216 | tf_op jit(solution)/shard_map/reshape | solution.py:36
  500.8 11.6 %copy.43 = f32[128,128,128]{1,2,0:T(8,128)} copy(f32[128,128,128]{1,0,2:T(8,128)} %bitcast.164) | data formatting | bytes 16777216 | tf_op jit(solution)/shard_map/transpose | solution.py:66
  512.5 10.3 %all-to-all-start.2 = ((f32[128,128,128]{1,2,0:T(8,128)}), f32[128,128,128]{1,2,0:T(8,128)}, u32[]{:S(2)}, u32[]{:S(2)}) async-start(f32[128,128,128]{1,2,0:T(8,128)} %copy.43), calls=%async_computation.2 | async-start | bytes 16777216 | tf_op jit(solution)/shard_map/all_to_all | solution.py:94
  522.7 4.2 shift-left_add_fusion.7
  527.0 0.2 fusion.24
  527.2 0.3 convolution_bitcast_fusion.9
  527.5 114.5 %all-to-all-done.2 = f32[128,128,128]{1,2,0:T(8,128)} async-done(((f32[128,128,128]{1,2,0:T(8,128)}), f32[128,128,128]{1,2,0:T(8,128)}, u32[]{:S(2)}, u32[]{:S(2)}) %all-to-all-start.2) | async-done | bytes 8388640 | tf_op jit(solution)/shard_map/all_to_all | solution.py:94
  642.1 9.3 %copy.44 = f32[128,128,128]{0,2,1:T(8,128)} copy(f32[128,128,128]{1,2,0:T(8,128)} %all-to-all-done.2) | data formatting | bytes 16777216 | tf_op jit(solution)/shard_map/all_to_all | solution.py:94
  651.4 10.3 %fusion.3 = f32[128,128,128]{2,0,1:T(8,128)S(1)} fusion(f32[128,128,1]{1,0,2:T(8,128)S(1)} %convolution_bitcast_fusion.9, f32[128,128,128]{0,2,1:T(8,128)} %copy.44), kind=kOutput, calls=%fused_computation.4 | convolution fusion | flops 3221225472 | bytes 16842752 | tf_op jit(solution)/shard_map/dot_general | solution.py:71
  661.7 4.9 copy.45
  666.6 110.2 %all_to_all.20 = f32[128,128,128]{2,1,0:T(8,128)S(1)} all-to-all(f32[128,128,128]{2,1,0:T(8,128)S(1)} %copy.45), channel_id=1, replica_groups=mesh['qa'=8,'qb'=16] {'qb'}, dimensions={0} | all-to-all | bytes 16777216 | tf_op jit(solution)/shard_map/all_to_all | solution.py:96
  776.8 3.4 copy.63
  (1 shorter events, 0.0 us)
Async XLA Ops:
  25.8 5.9 copy-start
  66.6 121.4 %all-to-all-start = ((f32[128,128,128]{2,1,0:T(8,128)}), f32[128,128,128]{2,1,0:T(8,128)}, u32[]{:S(2)}, u32[]{:S(2)}) async-start(f32[128,128,128]{2,1,0:T(8,128)} %fusion.5), calls=%async_computation | async-start | bytes 16777216 | tf_op jit(solution)/shard_map/all_to_all | solution.py:87
  229.1 5.1 copy-start.1
  229.1 119.8 %all-to-all-start.1 = ((f32[128,128,128]{2,1,0:T(8,128)}), f32[128,128,128]{2,1,0:T(8,128)}, u32[]{:S(2)}, u32[]{:S(2)}) async-start(f32[128,128,128]{2,1,0:T(8,128)} %copy.34), calls=%async_computation.1 | async-start | bytes 16777216 | tf_op jit(solution)/shard_map/all_to_all | solution.py:89
  512.5 129.6 %all-to-all-start.2 = ((f32[128,128,128]{1,2,0:T(8,128)}), f32[128,128,128]{1,2,0:T(8,128)}, u32[]{:S(2)}, u32[]{:S(2)}) async-start(f32[128,128,128]{1,2,0:T(8,128)} %copy.43), calls=%async_computation.2 | async-start | bytes 16777216 | tf_op jit(solution)/shard_map/all_to_all | solution.py:94
where the time goes:
time: 789 us; the launch traced here: 781 us
  waiting for transfers between devices  324 us (41%)
  local copies, waits for them, and re-layouts  168 us (21%)
  matrix products  122 us (15%)
  blocking collectives  110 us (14%)
  other arithmetic  34.7 us (4%)
  starting transfers between devices  21.7 us (3%)
    all_to_all x2, waiting for transfers between devices, on_device(): lax.all_to_all(state_grid, 'qa', split_axis=0, concat_axis=0, tiled=True)  210 us
    all_to_all x1, waiting for transfers between devices, on_device(): lax.all_to_all(state_grid, 'qb', split_axis=0, concat_axis=0, tiled=True)  115 us
    all_to_all x1, blocking collectives, on_device(): lax.all_to_all(state_grid, 'qb', split_axis=0, concat_axis=0, tiled=True)  110 us
    dot_general x4, matrix products, group_product(): jnp.einsum('ql,fln->fqn', gate_matrix, tiled_view, precision=lax.Precisio...  66.3 us
    add x8, other arithmetic, effective(): mapped + jnp.left_shift(jnp.bitwise_and(jnp.right_shift(basis_index, qubi...  34.7 us
    reshape x3, local copies, waits for them, and re-layouts, group_product(): return result.reshape(state_grid.shape)  27.8 us
    reshape x3, local copies, waits for them, and re-layouts, group_product(): tiled_view = state_grid.reshape(outer_size, extent, -1)  27.8 us
    transpose x3, local copies, waits for them, and re-layouts, group_product(): jnp.einsum('ql,fln->fqn', gate_matrix, tiled_view, precision=lax.Precisio...  27.5 us
  transfers between devices with their start and end apart: 3, of which 3 were waited for; matrix products, arithmetic and copies ran while one was open for 3% of the time, Pallas kernels for 0%

commit v1 on v0

v1 whole, which is shorter than its diff:
```python
import jax
import jax.numpy as jnp
from jax import lax
from jax.experimental import pallas as pl
from jax.experimental.pallas import tpu as pltpu
from jax.sharding import PartitionSpec as P

N = 128
BF = jnp.bfloat16
F32 = jnp.float32
F0, M0, B0, T0, F1, M1, B1, T1 = range(8)


def split(value, axis):
    high = value.astype(BF)
    low = (value - high.astype(F32)).astype(BF)
    return jnp.concatenate([high, low], axis=axis)


def turn(index, low_bits):
    return ((index & (2**low_bits - 1)) << (7 - low_bits)) | (index >> low_bits)


ROWS = {F1: 4, B1: 4, B0: 3}
COLUMNS = {F1: 4, B1: 4}


def gates_kernel(order_ref, gates_ref, stacked_ref):
    along = lax.broadcasted_iota(jnp.int32, (N, N), 0)
    across = lax.broadcasted_iota(jnp.int32, (N, N), 1)

    def mapped(index, slot):
        total = jnp.zeros_like(index)
        for k in range(7):
            total = total + (((index >> order_ref[slot, k]) & 1) << k)
        return total

    for slot in range(8):
        rows = turn(along, ROWS[slot]) if slot in ROWS else along
        columns = turn(across, COLUMNS[slot]) if slot in COLUMNS else across
        pick_rows = (mapped(rows, slot) == across).astype(F32).astype(BF)
        pick_columns = (mapped(columns, slot) == along).astype(F32).astype(BF)
        picked = jnp.dot(
            pick_rows, split(gates_ref[slot], 1), preferred_element_type=F32
        ).astype(BF)
        both = jnp.concatenate([picked[:, :N], picked[:, N:]], axis=0)
        effective = jnp.dot(both, pick_columns, preferred_element_type=F32).astype(BF)
        stacked_ref[slot] = jnp.concatenate([effective, effective], axis=1)


def stack_gates(gates, qubit_order):
    return pl.pallas_call(
        gates_kernel,
        out_shape=jax.ShapeDtypeStruct((8, 2 * N, 2 * N), BF),
        in_specs=[
            pl.BlockSpec(memory_space=pltpu.SMEM),
            pl.BlockSpec(memory_space=pltpu.VMEM),
        ],
        out_specs=pl.BlockSpec(memory_space=pltpu.VMEM),
        name="stack_gates",
    )(qubit_order.reshape(8, 7), gates.reshape(8, N, N))


def left(gate, blocks):
    width = len(blocks) * N
    value = jnp.concatenate(blocks, axis=1) if len(blocks) > 1 else blocks[0]
    both = jnp.dot(gate, split(value, 0), preferred_element_type=F32)
    total = both[:N] + both[N:]
    return [total[:, k : k + N] for k in range(0, width, N)]


def left_of_transposed(gate, blocks):
    width = len(blocks) * N
    value = jnp.concatenate(blocks, axis=0)
    both = lax.dot_general(
        gate, split(value, 1), (((1,), (1,)), ((), ())), preferred_element_type=F32
    )
    total = both[:N] + both[N:]
    return [total[:, k : k + N] for k in range(0, width, N)]


GROUP = 2


def before_kernel(x_ref, gates_ref, out_ref, held):
    step = pl.program_id(0)

    @pl.when(step < 16)
    def _():
        gate = gates_ref[M0]
        for k in range(0, 8, GROUP):
            done = left(gate, [x_ref[k + j] for j in range(GROUP)])
            for j in range(GROUP):
                start = pl.multiple_of((step * 8 + k + j) * N, N)
                held[pl.ds(start, N), :] = done[j]

    @pl.when(step >= 16)
    def _():
        gate = gates_ref[F0]
        b0 = step - 16
        for k in range(0, 8, GROUP):
            done = left(
                gate,
                [held[pl.ds(b0 + (k + j) * 16, N, stride=N), :] for j in range(GROUP)],
            )
            for j in range(GROUP):
                out_ref[:, 0, k + j] = done[j].reshape(8, 16, N)


def between_kernel(x_ref, gates_ref, out_ref, turned, held):
    step = pl.program_id(0)

    @pl.when(step < 16)
    def _():
        gate = gates_ref[T0]
        for k in range(0, 8, GROUP):
            done = left(
                gate, [x_ref[:, 0, k + j].reshape(N, N) for j in range(GROUP)]
            )
            for j in range(GROUP):
                turned[:, k + j] = done[j].reshape(8, 16, N)
        gate = gates_ref[F1]
        for k in range(0, 8, GROUP):
            done = left(gate, [turned[k + j].reshape(N, N) for j in range(GROUP)])
            for j in range(GROUP):
                held[k + j, step] = done[j].reshape(8, 16, N)

    @pl.when(step >= 16)
    def _():
        gate = gates_ref[T1]
        x = step - 16
        for b1 in range(8):
            done = left(
                gate, [held[x, :, b1, k : k + 8].reshape(N, N) for k in (0, 8)]
            )
            for j, k in enumerate((0, 8)):
                out_ref[0, :, b1, k : k + 8] = done[j].reshape(16, 8, N)


def after_kernel(x_ref, gates_ref, out_ref, turned, held, ready):
    step = pl.program_id(0)

    @pl.when(step < 8)
    def _():
        gate = gates_ref[B0]
        for k in range(0, 16, GROUP):
            done = left_of_transposed(
                gate, [x_ref[0, k + j].reshape(N, N) for j in range(GROUP)]
            )
            for j in range(GROUP):
                turned[:, k + j] = done[j].reshape(16, 8, N)
        gate = gates_ref[M1]
        for k in range(0, 16, GROUP):
            done = left(gate, [turned[k + j].reshape(N, N) for j in range(GROUP)])
            for j in range(GROUP):
                start = pl.multiple_of((step * 16 + k + j) * N, N)
                held[pl.ds(start, N), :] = done[j]

    @pl.when((step >= 8) & (step < 24))
    def _():
        gate = gates_ref[B1]
        b0 = step - 8
        for k in range(0, 8, GROUP):
            done = left(
                gate,
                [held[pl.ds(b0 * 8 + k + j, N, stride=N), :] for j in range(GROUP)],
            )
            for j in range(GROUP):
                ready[:, b0, k + j] = done[j].reshape(8, 16, N)

    @pl.when(step >= 24)
    def _():
        a1 = step - 24
        for b0 in range(16):
            block = ready[a1, b0].reshape(N, N).T
            for b1 in range(8):
                out_ref[pl.ds(b1 * 16 + b0, 16, stride=N), :] = block[
                    b1 * 16 : b1 * 16 + 16
                ]


VMEM_LIMIT = 60 * 2**20
WHOLE = pl.BlockSpec((8, 2 * N, 2 * N), lambda i: (0, 0, 0))


def before(state, stacked):
    return pl.pallas_call(
        before_kernel,
        grid=(32,),
        in_specs=[
            pl.BlockSpec((8, N, N), lambda i: (jnp.minimum(i, 15), 0, 0)),
            WHOLE,
        ],
        out_specs=pl.BlockSpec(
            (8, 1, 8, 16, N), lambda i: (0, jnp.maximum(i - 16, 0), 0, 0, 0)
        ),
        out_shape=jax.ShapeDtypeStruct((8, 16, 8, 16, N), F32),
        scratch_shapes=[pltpu.VMEM((N * N, N), F32)],
        compiler_params=pltpu.CompilerParams(vmem_limit_bytes=VMEM_LIMIT),
        name="before",
    )(state, stacked)


def between(state, stacked):
    return pl.pallas_call(
        between_kernel,
        grid=(24,),
        in_specs=[
            pl.BlockSpec(
                (8, 1, 8, 16, N), lambda i: (0, jnp.minimum(i, 15), 0, 0, 0)
            ),
            WHOLE,
        ],
        out_specs=pl.BlockSpec(
            (1, 16, 8, 16, N), lambda i: (jnp.maximum(i - 16, 0), 0, 0, 0, 0)
        ),
        out_shape=jax.ShapeDtypeStruct((8, 16, 8, 16, N), F32),
        scratch_shapes=[
            pltpu.VMEM((8, 8, 16, N), F32),
            pltpu.VMEM((8, 16, 8, 16, N), F32),
        ],
        compiler_params=pltpu.CompilerParams(vmem_limit_bytes=VMEM_LIMIT),
        name="between",
    )(state, stacked)


def after(state, stacked):
    return pl.pallas_call(
        after_kernel,
        grid=(32,),
        in_specs=[
            pl.BlockSpec(
                (1, 16, 8, 16, N), lambda i: (jnp.minimum(i, 7), 0, 0, 0, 0)
            ),
            WHOLE,
        ],
        out_specs=pl.BlockSpec(
            (16 * N, N), lambda i: (jnp.maximum(i - 24, 0), 0)
        ),
        out_shape=jax.ShapeDtypeStruct((N * N, N), F32),
        scratch_shapes=[
            pltpu.VMEM((16, 16, 8, N), F32),
            pltpu.VMEM((N * N, N), F32),
            pltpu.VMEM((8, 16, 8, 16, N), F32),
        ],
        compiler_params=pltpu.CompilerParams(vmem_limit_bytes=VMEM_LIMIT),
        name="after",
    )(state, stacked)


def exchange(state):
    sent = state.reshape(N, N, N)
    return lax.all_to_all(sent, ("qa", "qb"), 0, 0, tiled=True).reshape(state.shape)


def on_device(amplitudes, gates, qubit_order):
    stacked = stack_gates(gates, qubit_order)
    state = before(amplitudes.reshape(N, N, N), stacked)
    state = between(exchange(state), stacked)
    state = after(exchange(state), stacked)
    return state.reshape(amplitudes.shape)


def solution(mesh):
    return jax.shard_map(
        on_device,
        mesh=mesh,
        in_specs=(P("qa", "qb", None, None, None), P(), P()),
        out_specs=P("qa", "qb", None, None, None),
        check_vma=False,
    )
```

time: 789 us -> 292 us (0.37)
  waiting for transfers between devices: 324 us -> 0 us
  local copies, waits for them, and re-layouts: 168 us -> 0 us
  matrix products: 122 us -> 0 us
  blocking collectives: 110 us -> 217 us
  Pallas kernels: 0 us -> 73.8 us
  other arithmetic: 34.7 us -> 0 us
  starting transfers between devices: 21.7 us -> 0 us
    all_to_all x3 -> x0, waiting for transfers between devices: 324 us -> none  [the longest x2 210 us: on_device(): lax.all_to_all(state_grid, 'qa', split_axis=0, concat_axis=0, tiled=True)]
    dot_general x24 -> x0, matrix products: 122 us -> none  [the longest x4 66.3 us: group_product(): jnp.einsum('ql,fln->fqn', gate_matrix, tiled_view, precision=lax.Precisio...]
    all_to_all x1 -> x2, blocking collectives: 110 us -> 217 us  [exchange(): lax.all_to_all(sent, ('qa', 'qb'), 0, 0, tiled=True).reshape(state.shape)]
    pallas_call x0 -> x4, Pallas kernels: none -> 73.8 us  [the longest x1 26.8 us: after(): pl.pallas_call(after_kernel, grid=(32,), in_specs=[pl.BlockSpec((1, 16, 8...]
    reshape x6 -> x0, local copies, waits for them, and re-layouts: 55.6 us -> none  [the longest x3 27.8 us: group_product(): return result.reshape(state_grid.shape)]
    transpose x5 -> x0, local copies, waits for them, and re-layouts: 48.4 us -> none  [the longest x3 27.5 us: group_product(): jnp.einsum('ql,fln->fqn', gate_matrix, tiled_view, precision=lax.Precisio...]
    add x8 -> x0, other arithmetic: 34.7 us -> none  [effective(): mapped + jnp.left_shift(jnp.bitwise_and(jnp.right_shift(basis_index, qubi...]
    dot_general x3 -> x0, local copies, waits for them, and re-layouts: 22.1 us -> none  [apply_rows(): jnp.dot(gate_matrix, flattened, precision=lax.Precision.HIGHEST, preferre...]
  transfers between devices with their start and end apart: 3 -> 0, of which waited for: 3 -> 0; matrix products, arithmetic and copies ran while one was open for 3% -> 0% of each run, Pallas kernels for 0% -> 0%
where the time goes in v1:
time: 292 us; the launch traced here: 291 us
  blocking collectives  217 us (74%)
  Pallas kernels  73.8 us (25%)
    all_to_all x2, blocking collectives, exchange(): lax.all_to_all(sent, ('qa', 'qb'), 0, 0, tiled=True).reshape(state.shape)  217 us
    pallas_call x1, Pallas kernels, after(): pl.pallas_call(after_kernel, grid=(32,), in_specs=[pl.BlockSpec((1, 16, 8...  26.8 us
    pallas_call x1, Pallas kernels, before(): pl.pallas_call(before_kernel, grid=(32,), in_specs=[pl.BlockSpec((8, N, N...  23.4 us
    pallas_call x1, Pallas kernels, between(): pl.pallas_call(between_kernel, grid=(24,), in_specs=[pl.BlockSpec((8, 1,...  20.6 us

profile of v1, /device:TPU:1, one launch (start us, length us, event | category | flops | bytes accessed | tf_op | source)
XLA Modules:
  0.0 290.8 jit_solution(470309898033599608)
XLA Ops:
  0.0 3.0 %stack_gates.1.gates_ref = bf16[8,256,256]{2,1,0:T(8,128)(2,1)} custom-call(s32[8,7]{1,0:T(8,128)} %bitcast.14, f32[8,128,128]{2,1,0:T(8,128)} %bitcast.13), custom_call_target="tpu_custom_call" | custom-call | tf_op jit(solution)/shard_map/stack_gates/pallas_call | solution.py:52
  3.0 23.4 %before.1 = f32[8,16,8,16,128]{4,3,2,1,0:T(8,128)} custom-call(f32[128,128,128]{2,1,0:T(8,128)} %bitcast.12, bf16[8,256,256]{2,1,0:T(8,128)(2,1)} %stack_gates.1.gates_ref), custom_call_target="tpu_custom_call" | custom-call | tf_op jit(solution)/shard_map/before/pallas_call | solution.py:187
  26.4 110.6 %all_to_all.10 = f32[128,128,128]{2,1,0:T(8,128)} all-to-all(f32[128,128,128]{2,1,0:T(8,128)} %bitcast.11), channel_id=1, replica_groups=mesh['qa'=8,'qb'=16] {'qa','qb'}, dimensions={0} | all-to-all | bytes 16777216 | tf_op jit(solution)/shard_map/all_to_all | solution.py:253
  137.1 20.6 %between.1 = f32[8,16,8,16,128]{4,3,2,1,0:T(8,128)} custom-call(f32[8,16,8,16,128]{4,3,2,1,0:T(8,128)} %bitcast.9, bf16[8,256,256]{2,1,0:T(8,128)(2,1)} %stack_gates.1.gates_ref), custom_call_target="tpu_custom_call" | custom-call | tf_op jit(solution)/shard_map/between/pallas_call | solution.py:205
  157.6 106.4 %all_to_all.11 = f32[128,128,128]{2,1,0:T(8,128)} all-to-all(f32[128,128,128]{2,1,0:T(8,128)} %bitcast.10), channel_id=1, replica_groups=mesh['qa'=8,'qb'=16] {'qa','qb'}, dimensions={0} | all-to-all | bytes 16777216 | tf_op jit(solution)/shard_map/all_to_all | solution.py:253
  264.0 26.8 %after.1 = f32[16384,128]{1,0:T(8,128)} custom-call(f32[8,16,8,16,128]{4,3,2,1,0:T(8,128)} %bitcast.8, bf16[8,256,256]{2,1,0:T(8,128)(2,1)} %stack_gates.1.gates_ref), custom_call_target="tpu_custom_call" | custom-call | tf_op jit(solution)/shard_map/after/pallas_call | solution.py:228

commit v2 on v1

--- a/solution.py
+++ b/solution.py
@@ -80,119 +80,150 @@
 
 
 GROUP = 2
+STEPS = 4
 
 
 def before_kernel(x_ref, gates_ref, out_ref, held):
     step = pl.program_id(0)
 
-    @pl.when(step < 16)
+    @pl.when(step < STEPS)
     def _():
         gate = gates_ref[M0]
-        for k in range(0, 8, GROUP):
+        part = N // STEPS
+        for k in range(0, part, GROUP):
             done = left(gate, [x_ref[k + j] for j in range(GROUP)])
             for j in range(GROUP):
-                start = pl.multiple_of((step * 8 + k + j) * N, N)
+                start = pl.multiple_of((step * part + k + j) * N, N)
                 held[pl.ds(start, N), :] = done[j]
 
-    @pl.when(step >= 16)
+    @pl.when(step >= STEPS)
     def _():
         gate = gates_ref[F0]
-        b0 = step - 16
-        for k in range(0, 8, GROUP):
-            done = left(
-                gate,
-                [held[pl.ds(b0 + (k + j) * 16, N, stride=N), :] for j in range(GROUP)],
-            )
-            for j in range(GROUP):
-                out_ref[:, 0, k + j] = done[j].reshape(8, 16, N)
+        part = 16 // STEPS
+        for i in range(part):
+            b0 = (step - STEPS) * part + i
+            for k in range(0, 8, GROUP):
+                done = left(
+                    gate,
+                    [
+                        held[pl.ds(b0 + (k + j) * 16, N, stride=N), :]
+                        for j in range(GROUP)
+                    ],
+                )
+                for j in range(GROUP):
+                    out_ref[:, i, k + j] = done[j].reshape(8, 16, N)
 
 
 def between_kernel(x_ref, gates_ref, out_ref, turned, held):
     step = pl.program_id(0)
 
-    @pl.when(step < 16)
-    def _():
-        gate = gates_ref[T0]
-        for k in range(0, 8, GROUP):
-            done = left(
-                gate, [x_ref[:, 0, k + j].reshape(N, N) for j in range(GROUP)]
-            )
-            for j in range(GROUP):
-                turned[:, k + j] = done[j].reshape(8, 16, N)
-        gate = gates_ref[F1]
-        for k in range(0, 8, GROUP):
-            done = left(gate, [turned[k + j].reshape(N, N) for j in range(GROUP)])
-            for j in range(GROUP):
-                held[k + j, step] = done[j].reshape(8, 16, N)
-
-    @pl.when(step >= 16)
+    @pl.when(step < STEPS)
+    def _():
+        part = 16 // STEPS
+        for i in range(part):
+            gate = gates_ref[T0]
+            for k in range(0, 8, GROUP):
+                done = left(
+                    gate, [x_ref[:, i, k + j].reshape(N, N) for j in range(GROUP)]
+                )
+                for j in range(GROUP):
+                    turned[:, k + j] = done[j].reshape(8, 16, N)
+            gate = gates_ref[F1]
+            for k in range(0, 8, GROUP):
+                done = left(gate, [turned[k + j].reshape(N, N) for j in range(GROUP)])
+                for j in range(GROUP):
+                    held[k + j, step * part + i] = done[j].reshape(8, 16, N)
+
+    @pl.when(step >= STEPS)
     def _():
         gate = gates_ref[T1]
-        x = step - 16
-        for b1 in range(8):
-            done = left(
-                gate, [held[x, :, b1, k : k + 8].reshape(N, N) for k in (0, 8)]
-            )
-            for j, k in enumerate((0, 8)):
-                out_ref[0, :, b1, k : k + 8] = done[j].reshape(16, 8, N)
+        part = 8 // STEPS
+        for i in range(part):
+            x = (step - STEPS) * part + i
+            for b1 in range(8):
+                done = left(
+                    gate, [held[x, :, b1, k : k + 8].reshape(N, N) for k in (0, 8)]
+                )
+                for j, k in enumerate((0, 8)):
+                    out_ref[i, :, b1, k : k + 8] = done[j].reshape(16, 8, N)
 
 
 def after_kernel(x_ref, gates_ref, out_ref, turned, held, ready):
     step = pl.program_id(0)
 
-    @pl.when(step < 8)
-    def _():
-        gate = gates_ref[B0]
-        for k in range(0, 16, GROUP):
-            done = left_of_transposed(
-                gate, [x_ref[0, k + j].reshape(N, N) for j in range(GROUP)]
-            )
-            for j in range(GROUP):
-                turned[:, k + j] = done[j].reshape(16, 8, N)
-        gate = gates_ref[M1]
-        for k in range(0, 16, GROUP):
-            done = left(gate, [turned[k + j].reshape(N, N) for j in range(GROUP)])
-            for j in range(GROUP):
-                start = pl.multiple_of((step * 16 + k + j) * N, N)
-                held[pl.ds(start, N), :] = done[j]
-
-    @pl.when((step >= 8) & (step < 24))
+    @pl.when(step < STEPS)
+    def _():
+        part = 8 // STEPS
+        for i in range(part):
+            gate = gates_ref[B0]
+            for k in range(0, 16, GROUP):
+                done = left_of_transposed(
+                    gate, [x_ref[i, k + j].reshape(N, N) for j in range(GROUP)]
+                )
+                for j in range(GROUP):
+                    turned[:, k + j] = done[j].reshape(16, 8, N)
+            gate = gates_ref[M1]
+            for k in range(0, 16, GROUP):
+                done = left(gate, [turned[k + j].reshape(N, N) for j in range(GROUP)])
+                for j in range(GROUP):
+                    start = pl.multiple_of(
+                        ((step * part + i) * 16 + k + j) * N, N
+                    )
+                    held[pl.ds(start, N), :] = done[j]
+
+    @pl.when((step >= STEPS) & (step < 2 * STEPS))
     def _():
         gate = gates_ref[B1]
-        b0 = step - 8
-        for k in range(0, 8, GROUP):
-            done = left(
-                gate,
-                [held[pl.ds(b0 * 8 + k + j, N, stride=N), :] for j in range(GROUP)],
-            )
-            for j in range(GROUP):
-                ready[:, b0, k + j] = done[j].reshape(8, 16, N)
-
-    @pl.when(step >= 24)
-    def _():
-        a1 = step - 24
-        for b0 in range(16):
-            block = ready[a1, b0].reshape(N, N).T
-            for b1 in range(8):
-                out_ref[pl.ds(b1 * 16 + b0, 16, stride=N), :] = block[
-                    b1 * 16 : b1 * 16 + 16
-                ]
+        part = 16 // STEPS
+        for i in range(part):
+            b0 = (step - STEPS) * part + i
+            for k in range(0, 8, GROUP):
+                done = left(
+                    gate,
+                    [
+                        held[pl.ds(b0 * 8 + k + j, N, stride=N), :]
+                        for j in range(GROUP)
+                    ],
+                )
+                for j in range(GROUP):
+                    ready[:, b0, k + j] = done[j].reshape(8, 16, N)
+
+    @pl.when(step >= 2 * STEPS)
+    def _():
+        part = 8 // STEPS
+        for i in range(part):
+            a1 = (step - 2 * STEPS) * part + i
+            for b0 in range(16):
+                block = ready[a1, b0].reshape(N, N).T
+                for b1 in range(8):
+                    start = i * 16 * N + b1 * 16 + b0
+                    out_ref[pl.ds(start, 16, stride=N), :] = block[
+                        b1 * 16 : b1 * 16 + 16
+                    ]
 
 
 VMEM_LIMIT = 60 * 2**20
 WHOLE = pl.BlockSpec((8, 2 * N, 2 * N), lambda i: (0, 0, 0))
 
 
+def first(i):
+    return jnp.minimum(i, STEPS - 1)
+
+
+def last(i, earlier):
+    return jnp.maximum(i - earlier * STEPS, 0)
+
+
 def before(state, stacked):
     return pl.pallas_call(
         before_kernel,
-        grid=(32,),
-        in_specs=[
-            pl.BlockSpec((8, N, N), lambda i: (jnp.minimum(i, 15), 0, 0)),
+        grid=(2 * STEPS,),
+        in_specs=[
+            pl.BlockSpec((N // STEPS, N, N), lambda i: (first(i), 0, 0)),
             WHOLE,
         ],
         out_specs=pl.BlockSpec(
-            (8, 1, 8, 16, N), lambda i: (0, jnp.maximum(i - 16, 0), 0, 0, 0)
+            (8, 16 // STEPS, 8, 16, N), lambda i: (0, last(i, 1), 0, 0, 0)
         ),
         out_shape=jax.ShapeDtypeStruct((8, 16, 8, 16, N), F32),
         scratch_shapes=[pltpu.VMEM((N * N, N), F32)],
@@ -204,15 +235,13 @@
 def between(state, stacked):
     return pl.pallas_call(
         between_kernel,
-        grid=(24,),
-        in_specs=[
-            pl.BlockSpec(
-                (8, 1, 8, 16, N), lambda i: (0, jnp.minimum(i, 15), 0, 0, 0)
-            ),
+        grid=(2 * STEPS,),
+        in_specs=[
+            pl.BlockSpec((8, 16 // STEPS, 8, 16, N), lambda i: (0, first(i), 0, 0, 0)),
             WHOLE,
         ],
         out_specs=pl.BlockSpec(
-            (1, 16, 8, 16, N), lambda i: (jnp.maximum(i - 16, 0), 0, 0, 0, 0)
+            (8 // STEPS, 16, 8, 16, N), lambda i: (last(i, 1), 0, 0, 0, 0)
         ),
         out_shape=jax.ShapeDtypeStruct((8, 16, 8, 16, N), F32),
         scratch_shapes=[
@@ -227,16 +256,12 @@
 def after(state, stacked):
     return pl.pallas_call(
         after_kernel,
-        grid=(32,),
-        in_specs=[
-            pl.BlockSpec(
-                (1, 16, 8, 16, N), lambda i: (jnp.minimum(i, 7), 0, 0, 0, 0)
-            ),
+        grid=(3 * STEPS,),
+        in_specs=[
+            pl.BlockSpec((8 // STEPS, 16, 8, 16, N), lambda i: (first(i), 0, 0, 0, 0)),
             WHOLE,
         ],
-        out_specs=pl.BlockSpec(
-            (16 * N, N), lambda i: (jnp.maximum(i - 24, 0), 0)
-        ),
+        out_specs=pl.BlockSpec((16 // STEPS * 8 * N, N), lambda i: (last(i, 2), 0)),
         out_shape=jax.ShapeDtypeStruct((N * N, N), F32),
         scratch_shapes=[
             pltpu.VMEM((16, 16, 8, N), F32),

time: 292 us -> 271 us (0.928)
  Pallas kernels: 73.8 us -> 53.8 us
    pallas_call x3, Pallas kernels: 70.8 us -> 50.8 us  [the longest x1 22.2 us: after(): pl.pallas_call(after_kernel, grid=(3 * STEPS,), in_specs=[pl.BlockSpec((8...]
where the time goes in v2:
time: 271 us
  blocking collectives  217 us (80%)
  Pallas kernels  53.8 us (20%)
    all_to_all x2, blocking collectives, exchange(): lax.all_to_all(sent, ('qa', 'qb'), 0, 0, tiled=True).reshape(state.shape)  217 us
    pallas_call x1, Pallas kernels, after(): pl.pallas_call(after_kernel, grid=(3 * STEPS,), in_specs=[pl.BlockSpec((8...  22.2 us
    pallas_call x1, Pallas kernels, before(): pl.pallas_call(before_kernel, grid=(2 * STEPS,), in_specs=[pl.BlockSpec((...  14.5 us
    pallas_call x1, Pallas kernels, between(): pl.pallas_call(between_kernel, grid=(2 * STEPS,), in_specs=[pl.BlockSpec(...  14.1 us

profile of v2, /device:TPU:1, one launch (start us, length us, event | category | flops | bytes accessed | tf_op | source)
XLA Modules:
  0.0 270.8 jit_solution(2502367453160959344)
XLA Ops:
  0.0 3.0 %stack_gates.1.gates_ref = bf16[8,256,256]{2,1,0:T(8,128)(2,1)} custom-call(s32[8,7]{1,0:T(8,128)} %bitcast.14, f32[8,128,128]{2,1,0:T(8,128)} %bitcast.13), custom_call_target="tpu_custom_call" | custom-call | tf_op jit(solution)/shard_map/stack_gates/pallas_call | solution.py:52
  3.0 14.5 %before.1 = f32[8,16,8,16,128]{4,3,2,1,0:T(8,128)} custom-call(f32[128,128,128]{2,1,0:T(8,128)} %bitcast.12, bf16[8,256,256]{2,1,0:T(8,128)(2,1)} %stack_gates.1.gates_ref), custom_call_target="tpu_custom_call" | custom-call | tf_op jit(solution)/shard_map/before/pallas_call | solution.py:218
  17.5 110.6 %all_to_all.10 = f32[128,128,128]{2,1,0:T(8,128)} all-to-all(f32[128,128,128]{2,1,0:T(8,128)} %bitcast.11), channel_id=1, replica_groups=mesh['qa'=8,'qb'=16] {'qa','qb'}, dimensions={0} | all-to-all | bytes 16777216 | tf_op jit(solution)/shard_map/all_to_all | solution.py:278
  128.1 14.1 %between.1 = f32[8,16,8,16,128]{4,3,2,1,0:T(8,128)} custom-call(f32[8,16,8,16,128]{4,3,2,1,0:T(8,128)} %bitcast.9, bf16[8,256,256]{2,1,0:T(8,128)(2,1)} %stack_gates.1.gates_ref), custom_call_target="tpu_custom_call" | custom-call | tf_op jit(solution)/shard_map/between/pallas_call | solution.py:236
  142.2 106.4 %all_to_all.11 = f32[128,128,128]{2,1,0:T(8,128)} all-to-all(f32[128,128,128]{2,1,0:T(8,128)} %bitcast.10), channel_id=1, replica_groups=mesh['qa'=8,'qb'=16] {'qa','qb'}, dimensions={0} | all-to-all | bytes 16777216 | tf_op jit(solution)/shard_map/all_to_all | solution.py:278
  248.6 22.2 %after.1 = f32[16384,128]{1,0:T(8,128)} custom-call(f32[8,16,8,16,128]{4,3,2,1,0:T(8,128)} %bitcast.8, bf16[8,256,256]{2,1,0:T(8,128)(2,1)} %stack_gates.1.gates_ref), custom_call_target="tpu_custom_call" | custom-call | tf_op jit(solution)/shard_map/after/pallas_call | solution.py:257

commit v3 on v1

v3 whole, which is shorter than its diff:
```python
import jax
import jax.numpy as jnp
from jax import lax
from jax.experimental import pallas as pl
from jax.experimental.pallas import tpu as pltpu
from jax.sharding import PartitionSpec as P

N = 128
BF = jnp.bfloat16
F32 = jnp.float32
F0, M0, B0, T0, F1, M1, B1, T1 = range(8)
BEFORE, BETWEEN, AFTER = (M0, F0), (T0, F1, T1), (B0, M1, B1)


def split(value, axis):
    high = value.astype(BF)
    low = (value - high.astype(F32)).astype(BF)
    return jnp.concatenate([high, low], axis=axis)


def turn(index, low_bits):
    return ((index & (2**low_bits - 1)) << (7 - low_bits)) | (index >> low_bits)


ROWS = {F1: 4, B1: 4, B0: 3}
COLUMNS = {F1: 4, B1: 4}


def effective(slot, order_ref, gates_ref):
    along = lax.broadcasted_iota(jnp.int32, (N, N), 0)
    across = lax.broadcasted_iota(jnp.int32, (N, N), 1)

    def mapped(index):
        total = jnp.zeros_like(index)
        for k in range(7):
            total = total + (((index >> order_ref[slot, k]) & 1) << k)
        return total

    rows = turn(along, ROWS[slot]) if slot in ROWS else along
    columns = turn(across, COLUMNS[slot]) if slot in COLUMNS else across
    pick_rows = (mapped(rows) == across).astype(F32).astype(BF)
    pick_columns = (mapped(columns) == along).astype(F32).astype(BF)
    picked = jnp.dot(
        pick_rows, split(gates_ref[slot], 1), preferred_element_type=F32
    ).astype(BF)
    both = jnp.concatenate([picked[:, :N], picked[:, N:]], axis=0)
    parts = jnp.dot(both, pick_columns, preferred_element_type=F32).astype(BF)
    return jnp.concatenate([parts, parts], axis=1)


def left(gate, blocks):
    width = len(blocks) * N
    value = jnp.concatenate(blocks, axis=1) if len(blocks) > 1 else blocks[0]
    both = jnp.dot(gate, split(value, 0), preferred_element_type=F32)
    total = both[:N] + both[N:]
    return [total[:, k : k + N] for k in range(0, width, N)]


def left_of_transposed(gate, blocks):
    width = len(blocks) * N
    value = jnp.concatenate(blocks, axis=0)
    both = lax.dot_general(
        gate, split(value, 1), (((1,), (1,)), ((), ())), preferred_element_type=F32
    )
    total = both[:N] + both[N:]
    return [total[:, k : k + N] for k in range(0, width, N)]


GROUP = 2
STEPS = 4
ROW = N + 1


def before_kernel(
    x_ref, order_ref, gates_ref, out_ref, between_ref, after_ref, arrived, held, done_in
):
    part = N // STEPS

    def copy(i):
        rows = pl.ds(i * part, part)
        return pltpu.make_async_copy(x_ref.at[rows], arrived.at[rows], done_in.at[i])

    for i in range(STEPS):
        copy(i).start()
    for place, slot in enumerate(BETWEEN):
        between_ref[place] = effective(slot, order_ref, gates_ref)
    for place, slot in enumerate(AFTER):
        after_ref[place] = effective(slot, order_ref, gates_ref)

    middle = effective(M0, order_ref, gates_ref)
    front = effective(F0, order_ref, gates_ref)
    for i in range(STEPS):
        copy(i).wait()

        @pl.loop(0, part, step=16 * GROUP)
        def _(start):
            for k in range(0, 16 * GROUP, GROUP):
                a = i * part + start + k
                done = left(middle, [arrived[a + j] for j in range(GROUP)])
                for j in range(GROUP):
                    held[pl.ds((a + j) * ROW, N), :] = done[j]

    @pl.loop(0, 16, unroll=UNROLL)
    def _(b0):
        for k in range(0, 8, GROUP):
            done = left(
                front,
                [
                    held[pl.ds(b0 + (k + j) * 16, N, stride=ROW), :]
                    for j in range(GROUP)
                ],
            )
            for j in range(GROUP):
                out_ref[:, b0, k + j] = done[j].reshape(8, 16, N)


def between_kernel(x_ref, gates_ref, out_ref, turned, held):
    @pl.loop(0, 16, unroll=UNROLL)
    def _(y):
        gate = gates_ref[0]
        for k in range(0, 8, GROUP):
            done = left(gate, [x_ref[:, y, k + j].reshape(N, N) for j in range(GROUP)])
            for j in range(GROUP):
                turned[:, k + j] = done[j].reshape(8, 16, N)
        gate = gates_ref[1]
        for k in range(0, 8, GROUP):
            done = left(gate, [turned[k + j].reshape(N, N) for j in range(GROUP)])
            for j in range(GROUP):
                held[k + j, y] = done[j].reshape(8, 16, N)

    @pl.loop(0, 8, unroll=UNROLL)
    def _(x):
        gate = gates_ref[2]
        for b1 in range(8):
            done = left(
                gate, [held[x, :, b1, k : k + 8].reshape(N, N) for k in (0, 8)]
            )
            for j, k in enumerate((0, 8)):
                out_ref[x, :, b1, k : k + 8] = done[j].reshape(16, 8, N)


def after_kernel(x_ref, gates_ref, out_ref, turned, held, ready):
    step = pl.program_id(0)

    @pl.when(step == 0)
    def _():
        @pl.loop(0, 8, unroll=UNROLL)
        def _(a1):
            gate = gates_ref[0]
            for k in range(0, 16, GROUP):
                done = left_of_transposed(
                    gate, [x_ref[a1, k + j].reshape(N, N) for j in range(GROUP)]
                )
                for j in range(GROUP):
                    turned[:, k + j] = done[j].reshape(16, 8, N)
            gate = gates_ref[1]
            for k in range(0, 16, GROUP):
                done = left(gate, [turned[k + j].reshape(N, N) for j in range(GROUP)])
                for j in range(GROUP):
                    held[pl.ds((a1 * 16 + k + j) * ROW, N), :] = done[j]

        @pl.loop(0, 16, unroll=UNROLL)
        def _(b0):
            gate = gates_ref[2]
            for k in range(0, 8, GROUP):
                done = left(
                    gate,
                    [
                        held[pl.ds(b0 * 8 + k + j, N, stride=ROW), :]
                        for j in range(GROUP)
                    ],
                )
                for j in range(GROUP):
                    ready[:, b0, k + j] = done[j].reshape(8, 16, N)

    part = 8 // STEPS
    for i in range(part):
        for b0 in range(16):
            block = ready[step * part + i, b0].reshape(N, N).T
            for b1 in range(8):
                start = i * 16 * N + b1 * 16 + b0
                out_ref[pl.ds(start, 16, stride=N), :] = block[b1 * 16 : b1 * 16 + 16]


UNROLL = 8
IN_VMEM = pl.BlockSpec(memory_space=pltpu.VMEM)


def limit(mebibytes):
    return pltpu.CompilerParams(vmem_limit_bytes=mebibytes * 2**20)


def cost(gates):
    return pl.CostEstimate(
        flops=gates * 8 * N**4, bytes_accessed=2**24, transcendentals=0
    )


def before(state, gates, qubit_order):
    return pl.pallas_call(
        before_kernel,
        in_specs=[
            pl.BlockSpec(memory_space=pltpu.HBM),
            pl.BlockSpec(memory_space=pltpu.SMEM),
            IN_VMEM,
        ],
        out_specs=[IN_VMEM] * 3,
        out_shape=[
            pltpu.VMEM((8, 16, 8, 16, N), F32),
            pltpu.VMEM((len(BETWEEN), 2 * N, 2 * N), BF),
            pltpu.VMEM((len(AFTER), 2 * N, 2 * N), BF),
        ],
        scratch_shapes=[
            pltpu.VMEM((N, N, N), F32),
            pltpu.VMEM((N * ROW, N), F32),
            pltpu.SemaphoreType.DMA((STEPS,)),
        ],
        compiler_params=limit(24),
        cost_estimate=cost(2),
        name="before",
    )(
        pltpu.with_memory_space_constraint(state, pltpu.HBM),
        qubit_order.reshape(8, 7),
        gates.reshape(8, N, N),
    )


def between(state, stacked):
    return pl.pallas_call(
        between_kernel,
        in_specs=[IN_VMEM, IN_VMEM],
        out_specs=IN_VMEM,
        out_shape=pltpu.VMEM((8, 16, 8, 16, N), F32),
        scratch_shapes=[
            pltpu.VMEM((8, 8, 16, N), F32),
            pltpu.VMEM((8, 16, 8, 16, N), F32),
        ],
        compiler_params=limit(24),
        cost_estimate=cost(3),
        name="between",
    )(
        pltpu.with_memory_space_constraint(state, pltpu.VMEM),
        pltpu.with_memory_space_constraint(stacked, pltpu.VMEM),
    )


def after(state, stacked):
    return pl.pallas_call(
        after_kernel,
        grid=(STEPS,),
        in_specs=[IN_VMEM, IN_VMEM],
        out_specs=pl.BlockSpec((N // STEPS * N, N), lambda i: (i, 0)),
        out_shape=jax.ShapeDtypeStruct((N * N, N), F32),
        scratch_shapes=[
            pltpu.VMEM((16, 16, 8, N), F32),
            pltpu.VMEM((N * ROW, N), F32),
            pltpu.VMEM((8, 16, 8, 16, N), F32),
        ],
        compiler_params=limit(32),
        cost_estimate=cost(3),
        name="after",
    )(
        pltpu.with_memory_space_constraint(state, pltpu.VMEM),
        pltpu.with_memory_space_constraint(stacked, pltpu.VMEM),
    )


def exchange(state):
    sent = state.reshape(N, N, N)
    return lax.all_to_all(sent, ("qa", "qb"), 0, 0, tiled=True).reshape(state.shape)


def on_device(amplitudes, gates, qubit_order):
    state, in_between, at_end = before(
        amplitudes.reshape(N, N, N), gates, qubit_order
    )
    state = between(exchange(state), in_between)
    state = after(exchange(state), at_end)
    return state.reshape(amplitudes.shape)


def solution(mesh):
    return jax.shard_map(
        on_device,
        mesh=mesh,
        in_specs=(P("qa", "qb", None, None, None), P(), P()),
        out_specs=P("qa", "qb", None, None, None),
        check_vma=False,
    )
```

time: 292 us -> 251 us (0.86)
  Pallas kernels: 73.8 us -> 32.8 us
    pallas_call x4 -> x3, Pallas kernels: 73.8 us -> 32.8 us  [the longest x1 15.4 us: after(): pl.pallas_call(after_kernel, grid=(STEPS,), in_specs=[IN_VMEM, IN_VMEM],...]
where the time goes in v3:
time: 251 us
  blocking collectives  216 us (86%)
  Pallas kernels  32.8 us (13%)
    all_to_all x2, blocking collectives, exchange(): lax.all_to_all(sent, ('qa', 'qb'), 0, 0, tiled=True).reshape(state.shape)  216 us
    pallas_call x1, Pallas kernels, after(): pl.pallas_call(after_kernel, grid=(STEPS,), in_specs=[IN_VMEM, IN_VMEM],...  15.4 us
    pallas_call x1, Pallas kernels, between(): pl.pallas_call(between_kernel, in_specs=[IN_VMEM, IN_VMEM], out_specs=IN_...  9.37 us
    pallas_call x1, Pallas kernels, before(): pl.pallas_call(before_kernel, in_specs=[pl.BlockSpec(memory_space=pltpu.H...  8.05 us

profile of v3, /device:TPU:1, one launch (start us, length us, event | category | flops | bytes accessed | tf_op | source)
XLA Modules:
  0.0 251.0 jit_solution(16075702013651576402)
XLA Ops:
  0.0 0.0 copy-start
  0.0 1.0 copy-done
  1.0 0.0 copy-start.1
  1.0 0.7 copy-done.1
  1.7 8.1 %before.1 = (f32[8,16,8,16,128]{4,3,2,1,0:T(8,128)S(1)}, bf16[3,256,256]{2,1,0:T(8,128)(2,1)S(1)}, bf16[3,256,256]{2,1,0:T(8,128)(2,1)S(1)}) custom-call(f32[128,128,128]{2,1,0:T(8,128)} %bitcast.14, s32[8,7]{1,0:T(8,128)S(1)} %bitcast.13, f32[8,128,128]{2,1,0:T(8,128)S(1)} %bitcast.12), custom_call_target="tpu_custom_call" | custom-call | flops 4294967296 | bytes 16777216 | tf_op jit(solution)/shard_map/before/pallas_call | solution.py:200
  9.8 110.3 %all_to_all.10 = f32[128,128,128]{2,1,0:T(8,128)S(1)} all-to-all(f32[128,128,128]{2,1,0:T(8,128)S(1)} %bitcast.8), channel_id=1, replica_groups=mesh['qa'=8,'qb'=16] {'qa','qb'}, dimensions={0} | all-to-all | bytes 16777216 | tf_op jit(solution)/shard_map/all_to_all | solution.py:270
  120.1 9.4 %between.1 = f32[8,16,8,16,128]{4,3,2,1,0:T(8,128)S(1)} custom-call(f32[8,16,8,16,128]{4,3,2,1,0:T(8,128)S(1)} %bitcast.10, bf16[3,256,256]{2,1,0:T(8,128)(2,1)S(1)} %get-tuple-element.9.gates_ref), custom_call_target="tpu_custom_call" | custom-call | flops 6442450944 | bytes 16777216 | tf_op jit(solution)/shard_map/between/pallas_call | solution.py:229
  129.5 106.1 %all_to_all.11 = f32[128,128,128]{2,1,0:T(8,128)S(1)} all-to-all(f32[128,128,128]{2,1,0:T(8,128)S(1)} %bitcast.11), channel_id=1, replica_groups=mesh['qa'=8,'qb'=16] {'qa','qb'}, dimensions={0} | all-to-all | bytes 16777216 | tf_op jit(solution)/shard_map/all_to_all | solution.py:270
  235.6 15.4 %after.1 = f32[16384,128]{1,0:T(8,128)} custom-call(f32[8,16,8,16,128]{4,3,2,1,0:T(8,128)S(1)} %bitcast.9, bf16[3,256,256]{2,1,0:T(8,128)(2,1)S(1)} %get-tuple-element.10.gates_ref), custom_call_target="tpu_custom_call" | custom-call | flops 6442450944 | bytes 16777216 | tf_op jit(solution)/shard_map/after/pallas_call | solution.py:248
Async XLA Ops:
  0.0 1.0 copy-start
  1.0 0.7 copy-start.1

commit v4 on v3

--- a/solution.py
+++ b/solution.py
@@ -68,11 +68,23 @@
 
 GROUP = 2
 STEPS = 4
+PIECES = 8
 ROW = N + 1
+LINE = N + 8
 
 
 def before_kernel(
-    x_ref, order_ref, gates_ref, out_ref, between_ref, after_ref, arrived, held, done_in
+    x_ref,
+    order_hbm,
+    gates_hbm,
+    out_ref,
+    between_ref,
+    after_ref,
+    order_ref,
+    gates_ref,
+    arrived,
+    held,
+    done_in,
 ):
     part = N // STEPS
 
@@ -80,8 +92,16 @@
         rows = pl.ds(i * part, part)
         return pltpu.make_async_copy(x_ref.at[rows], arrived.at[rows], done_in.at[i])
 
+    small = [
+        pltpu.make_async_copy(order_hbm, order_ref, done_in.at[STEPS]),
+        pltpu.make_async_copy(gates_hbm, gates_ref, done_in.at[STEPS + 1]),
+    ]
+    for one in small:
+        one.start()
     for i in range(STEPS):
         copy(i).start()
+    for one in small:
+        one.wait()
     for place, slot in enumerate(BETWEEN):
         between_ref[place] = effective(slot, order_ref, gates_ref)
     for place, slot in enumerate(AFTER):
@@ -139,47 +159,57 @@
                 out_ref[x, :, b1, k : k + 8] = done[j].reshape(16, 8, N)
 
 
-def after_kernel(x_ref, gates_ref, out_ref, turned, held, ready):
-    step = pl.program_id(0)
-
-    @pl.when(step == 0)
-    def _():
-        @pl.loop(0, 8, unroll=UNROLL)
-        def _(a1):
-            gate = gates_ref[0]
-            for k in range(0, 16, GROUP):
-                done = left_of_transposed(
-                    gate, [x_ref[a1, k + j].reshape(N, N) for j in range(GROUP)]
-                )
-                for j in range(GROUP):
-                    turned[:, k + j] = done[j].reshape(16, 8, N)
-            gate = gates_ref[1]
-            for k in range(0, 16, GROUP):
-                done = left(gate, [turned[k + j].reshape(N, N) for j in range(GROUP)])
-                for j in range(GROUP):
-                    held[pl.ds((a1 * 16 + k + j) * ROW, N), :] = done[j]
-
-        @pl.loop(0, 16, unroll=UNROLL)
-        def _(b0):
-            gate = gates_ref[2]
-            for k in range(0, 8, GROUP):
-                done = left(
-                    gate,
-                    [
-                        held[pl.ds(b0 * 8 + k + j, N, stride=ROW), :]
-                        for j in range(GROUP)
-                    ],
-                )
-                for j in range(GROUP):
-                    ready[:, b0, k + j] = done[j].reshape(8, 16, N)
-
-    part = 8 // STEPS
-    for i in range(part):
-        for b0 in range(16):
-            block = ready[step * part + i, b0].reshape(N, N).T
-            for b1 in range(8):
-                start = i * 16 * N + b1 * 16 + b0
-                out_ref[pl.ds(start, 16, stride=N), :] = block[b1 * 16 : b1 * 16 + 16]
+def after_kernel(x_ref, gates_ref, out_ref, turned, held, ready, lines, done_out):
+    @pl.loop(0, 8, unroll=UNROLL)
+    def _(a1):
+        gate = gates_ref[0]
+        for k in range(0, 16, GROUP):
+            done = left_of_transposed(
+                gate, [x_ref[a1, k + j].reshape(N, N) for j in range(GROUP)]
+            )
+            for j in range(GROUP):
+                turned[:, k + j] = done[j].reshape(16, 8, N)
+        gate = gates_ref[1]
+        for k in range(0, 16, GROUP):
+            done = left(gate, [turned[k + j].reshape(N, N) for j in range(GROUP)])
+            for j in range(GROUP):
+                held[pl.ds((a1 * 16 + k + j) * ROW, N), :] = done[j]
+
+    @pl.loop(0, 16, unroll=UNROLL)
+    def _(b0):
+        gate = gates_ref[2]
+        for k in range(0, 8, GROUP):
+            done = left(
+                gate,
+                [
+                    held[pl.ds(b0 * 8 + k + j, N, stride=ROW), :]
+                    for j in range(GROUP)
+                ],
+            )
+            for j in range(GROUP):
+                ready[:, b0, k + j] = done[j].reshape(8, 16, N)
+
+    def copy(i):
+        part = N // PIECES
+        return pltpu.make_async_copy(
+            lines.reshape(N, LINE, N).at[pl.ds(i * part, part), pl.ds(0, N)],
+            out_ref.at[pl.ds(i * part, part)],
+            done_out.at[i],
+        )
+
+    part = 8 // PIECES
+    for i in range(PIECES):
+        for a1 in range(i * part, i * part + part):
+            for b0 in range(16):
+                block = ready[a1, b0].reshape(N, N).T
+                for b1 in range(8):
+                    start = a1 * 16 * LINE + b1 * 16 + b0
+                    lines[pl.ds(start, 16, stride=LINE), :] = block[
+                        b1 * 16 : b1 * 16 + 16
+                    ]
+        copy(i).start()
+    for i in range(PIECES):
+        copy(i).wait()
 
 
 UNROLL = 8
@@ -199,11 +229,7 @@
 def before(state, gates, qubit_order):
     return pl.pallas_call(
         before_kernel,
-        in_specs=[
-            pl.BlockSpec(memory_space=pltpu.HBM),
-            pl.BlockSpec(memory_space=pltpu.SMEM),
-            IN_VMEM,
-        ],
+        in_specs=[pl.BlockSpec(memory_space=pltpu.HBM)] * 3,
         out_specs=[IN_VMEM] * 3,
         out_shape=[
             pltpu.VMEM((8, 16, 8, 16, N), F32),
@@ -211,17 +237,19 @@
             pltpu.VMEM((len(AFTER), 2 * N, 2 * N), BF),
         ],
         scratch_shapes=[
+            pltpu.SMEM((8, 7), jnp.int32),
+            pltpu.VMEM((8, N, N), F32),
             pltpu.VMEM((N, N, N), F32),
             pltpu.VMEM((N * ROW, N), F32),
-            pltpu.SemaphoreType.DMA((STEPS,)),
+            pltpu.SemaphoreType.DMA((STEPS + 2,)),
         ],
         compiler_params=limit(24),
         cost_estimate=cost(2),
         name="before",
     )(
         pltpu.with_memory_space_constraint(state, pltpu.HBM),
-        qubit_order.reshape(8, 7),
-        gates.reshape(8, N, N),
+        pltpu.with_memory_space_constraint(qubit_order.reshape(8, 7), pltpu.HBM),
+        pltpu.with_memory_space_constraint(gates.reshape(8, N, N), pltpu.HBM),
     )
 
 
@@ -247,16 +275,17 @@
 def after(state, stacked):
     return pl.pallas_call(
         after_kernel,
-        grid=(STEPS,),
         in_specs=[IN_VMEM, IN_VMEM],
-        out_specs=pl.BlockSpec((N // STEPS * N, N), lambda i: (i, 0)),
-        out_shape=jax.ShapeDtypeStruct((N * N, N), F32),
+        out_specs=pl.BlockSpec(memory_space=pltpu.HBM),
+        out_shape=pltpu.HBM((N, N, N), F32),
         scratch_shapes=[
             pltpu.VMEM((16, 16, 8, N), F32),
             pltpu.VMEM((N * ROW, N), F32),
             pltpu.VMEM((8, 16, 8, 16, N), F32),
+            pltpu.VMEM((N * LINE, N), F32),
+            pltpu.SemaphoreType.DMA((PIECES,)),
         ],
-        compiler_params=limit(32),
+        compiler_params=limit(36),
         cost_estimate=cost(3),
         name="after",
     )(

time: 251 us -> 245 us (0.976)
  Pallas kernels: 32.8 us -> 28.5 us
    pallas_call x1, Pallas kernels: 15.4 us -> 11.8 us  [after(): pl.pallas_call(after_kernel, in_specs=[IN_VMEM, IN_VMEM], out_specs=pl.Bl...]
where the time goes in v4:
time: 245 us
  blocking collectives  216 us (88%)
  Pallas kernels  28.5 us (12%)
    all_to_all x2, blocking collectives, exchange(): lax.all_to_all(sent, ('qa', 'qb'), 0, 0, tiled=True).reshape(state.shape)  216 us
    pallas_call x1, Pallas kernels, after(): pl.pallas_call(after_kernel, in_specs=[IN_VMEM, IN_VMEM], out_specs=pl.Bl...  11.8 us
    pallas_call x1, Pallas kernels, between(): pl.pallas_call(between_kernel, in_specs=[IN_VMEM, IN_VMEM], out_specs=IN_...  9.26 us
    pallas_call x1, Pallas kernels, before(): pl.pallas_call(before_kernel, in_specs=[pl.BlockSpec(memory_space=pltpu.H...  7.41 us

profile of v4, /device:TPU:1, one launch (start us, length us, event | category | flops | bytes accessed | tf_op | source)
XLA Modules:
  0.0 245.1 jit_solution(15103173808256681010)
XLA Ops:
  0.0 7.4 %before.1 = (f32[8,16,8,16,128]{4,3,2,1,0:T(8,128)S(1)}, bf16[3,256,256]{2,1,0:T(8,128)(2,1)S(1)}, bf16[3,256,256]{2,1,0:T(8,128)(2,1)S(1)}) custom-call(f32[128,128,128]{2,1,0:T(8,128)} %bitcast.12, s32[8,7]{1,0:T(8,128)} %bitcast.14, f32[8,128,128]{2,1,0:T(8,128)} %bitcast.13), custom_call_target="tpu_custom_call" | custom-call | flops 4294967296 | bytes 16777216 | tf_op jit(solution)/shard_map/before/pallas_call | solution.py:230
  7.4 110.3 %all_to_all.10 = f32[128,128,128]{2,1,0:T(8,128)S(1)} all-to-all(f32[128,128,128]{2,1,0:T(8,128)S(1)} %bitcast.8), channel_id=1, replica_groups=mesh['qa'=8,'qb'=16] {'qa','qb'}, dimensions={0} | all-to-all | bytes 16777216 | tf_op jit(solution)/shard_map/all_to_all | solution.py:299
  117.8 9.3 %between.1 = f32[8,16,8,16,128]{4,3,2,1,0:T(8,128)S(1)} custom-call(f32[8,16,8,16,128]{4,3,2,1,0:T(8,128)S(1)} %bitcast.10, bf16[3,256,256]{2,1,0:T(8,128)(2,1)S(1)} %get-tuple-element.9.gates_ref), custom_call_target="tpu_custom_call" | custom-call | flops 6442450944 | bytes 16777216 | tf_op jit(solution)/shard_map/between/pallas_call | solution.py:257
  127.0 106.1 %all_to_all.11 = f32[128,128,128]{2,1,0:T(8,128)S(1)} all-to-all(f32[128,128,128]{2,1,0:T(8,128)S(1)} %bitcast.11), channel_id=1, replica_groups=mesh['qa'=8,'qb'=16] {'qa','qb'}, dimensions={0} | all-to-all | bytes 16777216 | tf_op jit(solution)/shard_map/all_to_all | solution.py:299
  233.1 11.8 %after.1 = f32[128,128,128]{2,1,0:T(8,128)} custom-call(f32[8,16,8,16,128]{4,3,2,1,0:T(8,128)S(1)} %bitcast.9, bf16[3,256,256]{2,1,0:T(8,128)(2,1)S(1)} %get-tuple-element.10.gates_ref), custom_call_target="tpu_custom_call" | custom-call | flops 6442450944 | bytes 16777216 | tf_op jit(solution)/shard_map/after/pallas_call | solution.py:276

commit v5 on v4

--- a/solution.py
+++ b/solution.py
@@ -51,8 +51,10 @@
 def left(gate, blocks):
     width = len(blocks) * N
     value = jnp.concatenate(blocks, axis=1) if len(blocks) > 1 else blocks[0]
-    both = jnp.dot(gate, split(value, 0), preferred_element_type=F32)
-    total = both[:N] + both[N:]
+    parts = split(value, 0)
+    total = jnp.dot(gate[:N], parts, preferred_element_type=F32) + jnp.dot(
+        gate[N:, :N], parts[:N], preferred_element_type=F32
+    )
     return [total[:, k : k + N] for k in range(0, width, N)]
 
 

time: 245 us -> 245 us (level)
  no operation moved by 1% of the time
where the time goes in v5:
time: 245 us
  blocking collectives  216 us (88%)
  Pallas kernels  28.6 us (12%)
    all_to_all x2, blocking collectives, exchange(): lax.all_to_all(sent, ('qa', 'qb'), 0, 0, tiled=True).reshape(state.shape)  216 us
    pallas_call x1, Pallas kernels, after(): pl.pallas_call(after_kernel, in_specs=[IN_VMEM, IN_VMEM], out_specs=pl.Bl...  12.1 us
    pallas_call x1, Pallas kernels, between(): pl.pallas_call(between_kernel, in_specs=[IN_VMEM, IN_VMEM], out_specs=IN_...  9.04 us
    pallas_call x1, Pallas kernels, before(): pl.pallas_call(before_kernel, in_specs=[pl.BlockSpec(memory_space=pltpu.H...  7.4 us

profile of v5, /device:TPU:1, one launch (start us, length us, event | category | flops | bytes accessed | tf_op | source)
XLA Modules:
  0.0 245.2 jit_solution(696691598084875661)
XLA Ops:
  0.0 7.4 %before.1 = (f32[8,16,8,16,128]{4,3,2,1,0:T(8,128)S(1)}, bf16[3,256,256]{2,1,0:T(8,128)(2,1)S(1)}, bf16[3,256,256]{2,1,0:T(8,128)(2,1)S(1)}) custom-call(f32[128,128,128]{2,1,0:T(8,128)} %bitcast.12, s32[8,7]{1,0:T(8,128)} %bitcast.14, f32[8,128,128]{2,1,0:T(8,128)} %bitcast.13), custom_call_target="tpu_custom_call" | custom-call | flops 4294967296 | bytes 16777216 | tf_op jit(solution)/shard_map/before/pallas_call | solution.py:232
  7.4 110.3 %all_to_all.10 = f32[128,128,128]{2,1,0:T(8,128)S(1)} all-to-all(f32[128,128,128]{2,1,0:T(8,128)S(1)} %bitcast.8), channel_id=1, replica_groups=mesh['qa'=8,'qb'=16] {'qa','qb'}, dimensions={0} | all-to-all | bytes 16777216 | tf_op jit(solution)/shard_map/all_to_all | solution.py:301
  117.7 9.0 %between.1 = f32[8,16,8,16,128]{4,3,2,1,0:T(8,128)S(1)} custom-call(f32[8,16,8,16,128]{4,3,2,1,0:T(8,128)S(1)} %bitcast.10, bf16[3,256,256]{2,1,0:T(8,128)(2,1)S(1)} %get-tuple-element.9.gates_ref), custom_call_target="tpu_custom_call" | custom-call | flops 6442450944 | bytes 16777216 | tf_op jit(solution)/shard_map/between/pallas_call | solution.py:259
  126.8 106.1 %all_to_all.11 = f32[128,128,128]{2,1,0:T(8,128)S(1)} all-to-all(f32[128,128,128]{2,1,0:T(8,128)S(1)} %bitcast.11), channel_id=1, replica_groups=mesh['qa'=8,'qb'=16] {'qa','qb'}, dimensions={0} | all-to-all | bytes 16777216 | tf_op jit(solution)/shard_map/all_to_all | solution.py:301
  232.9 12.1 %after.1 = f32[128,128,128]{2,1,0:T(8,128)} custom-call(f32[8,16,8,16,128]{4,3,2,1,0:T(8,128)S(1)} %bitcast.9, bf16[3,256,256]{2,1,0:T(8,128)(2,1)S(1)} %get-tuple-element.10.gates_ref), custom_call_target="tpu_custom_call" | custom-call | flops 6442450944 | bytes 16777216 | tf_op jit(solution)/shard_map/after/pallas_call | solution.py:278
